TPU v7x, 512 devices: a whole 4x4x16 slice. The times are simulated.
512 devices in a mesh: ctx: 16 (over z_lo, core), exp: 32 (over z_hi, x, y).
Axes of the slice: x: 4, y: 4, z: 16 (z_hi: 2, z_lo: 8; z = z_hi * 8 + z_lo), core: 2. Of those that a mesh axis runs over, the one named last changes fastest.
Arguments:
- query: bfloat16 [32, 2048, 4096], P('exp', 'ctx'), may hold values from -41 to 41
- keyval: bfloat16 [32, 2, 2048, 256], P('exp', None, 'ctx'), may hold values from -4 to 4
- doc_ids: int32 [32, 2048], P('exp', 'ctx'), may hold values from 0 to 5, never falling along the last dimension, each value on 1 to 1024 neighbouring positions
- route_ids: int32 [32, 2048], P('exp', 'ctx'), may hold values from 0 to 63
- combine: float32 [32, 2048], P('exp', 'ctx'), may hold values from 0.5 to 2
- w_gate_up: bfloat16 [32, 2, 1536, 4096], P('exp', None, 'ctx'), may hold values from -0.09375 to 0.09375
- w_down: bfloat16 [32, 1536, 4096], P('exp', None, 'ctx'), may hold values from -0.15625 to 0.15625
Outputs:
- layer_out: bfloat16 [32, 2048, 4096], P('exp', 'ctx')
All inputs are finite; a program needn't handle non-finite values.
Results may differ from a plain program's by a relative error of at most 0.024.
Values may be sent and summed in bfloat16 or wider, within the bound.
A program may use at most 128 MiB of HBM per device.

v0:
```python
import jax
import jax.numpy as jnp
from jax import lax
from jax.sharding import PartitionSpec as P

HD = 128
CAP = 2
neg_large = -1e30
norm_eps = 1e-06


def shifted(value, axis, by):
    length = lax.axis_size(axis)
    return lax.ppermute(value, axis, [(i, (i + by) % length) for i in range(length)])


def shards(query, keyval, doc_ids, route_ids, combine, w_gate_up, w_down):
    tok_rows = query.shape[1]
    feature_width = query.shape[2]
    kv_heads = keyval.shape[3] // HD
    head_group = feature_width // HD // kv_heads
    ctx_count = lax.axis_size("ctx")
    q_heads = query[0].reshape(tok_rows, kv_heads, head_group, HD)
    q_doc = doc_ids[0]
    score_scale = HD ** (-0.5)

    def attend(loop_carry, kv_pair):
        kv_piece, doc_piece = kv_pair
        rows_here = kv_piece.shape[2]
        key_rows = kv_piece[0, 0].reshape(rows_here, kv_heads, HD)
        value_rows = kv_piece[0, 1].reshape(rows_here, kv_heads, HD)
        allowed = doc_piece[0, 0][None, :] == q_doc[:, None]
        running_max, running_sum, running_out = loop_carry
        scores = (
            jnp.einsum("qhgd,khd->hgqk", q_heads, key_rows, preferred_element_type=jnp.float32)
            * score_scale
        )
        masked = jnp.where(allowed, scores, neg_large)
        fresh_max = jnp.maximum(running_max, jnp.max(masked, axis=-1))
        prob_block = jnp.where(allowed, jnp.exp(masked - fresh_max[..., None]), 0.0)
        rescale = jnp.exp(running_max - fresh_max)
        running_sum = running_sum * rescale + jnp.sum(prob_block, axis=-1)
        block_out = jnp.einsum(
            "hgqk,khd->hgqd",
            prob_block.astype(jnp.bfloat16),
            value_rows,
            preferred_element_type=jnp.float32,
        )
        return (fresh_max, running_sum, running_out * rescale[..., None] + block_out)

    start_state = (
        jnp.full((kv_heads, head_group, tok_rows), neg_large, jnp.float32),
        jnp.zeros((kv_heads, head_group, tok_rows), jnp.float32),
        jnp.zeros((kv_heads, head_group, tok_rows, HD), jnp.float32),
    )
    doc_keys = doc_ids.reshape(1, 1, tok_rows)

    def cycle_step(step_index, loop_state):
        loop_carry, kv_now, doc_now = loop_state
        loop_carry = attend(loop_carry, (kv_now, doc_now))
        kv_next, doc_next = shifted((kv_now, doc_now), "ctx", 1)
        return (loop_carry, kv_next, doc_next)

    loop_carry, kv_last, doc_last = lax.fori_loop(
        0, ctx_count - 1, cycle_step, (start_state, keyval, doc_keys)
    )
    running_max, running_sum, running_out = attend(loop_carry, (kv_last, doc_last))
    head_major = (running_out / running_sum[..., None]).astype(jnp.bfloat16)
    attended = head_major.transpose(2, 0, 1, 3).reshape(tok_rows, feature_width)
    flat_attended = attended.astype(jnp.float32)
    normed = (
        flat_attended
        * lax.rsqrt(jnp.mean(flat_attended * flat_attended, axis=-1, keepdims=True) + norm_eps)
    ).astype(jnp.bfloat16)
    expert_count = lax.axis_size("exp")
    token_ids = route_ids[0]
    onehot = (token_ids[:, None] == lax.iota(jnp.int32, expert_count)[None, :]).astype(jnp.int32)
    earlier = jnp.sum((jnp.cumsum(onehot, axis=0) - onehot) * onehot, axis=1)
    kept = (token_ids < expert_count) & (earlier < CAP)
    slot = jnp.where(kept, token_ids * CAP + earlier, -1)
    chooser = (lax.iota(jnp.int32, expert_count * CAP)[:, None] == slot[None, :]).astype(
        jnp.bfloat16
    )
    outgoing = jnp.dot(chooser, normed, preferred_element_type=jnp.float32).astype(jnp.bfloat16)
    outgoing = outgoing.reshape(expert_count, CAP, feature_width)
    arrived = lax.all_to_all(outgoing, "exp", split_axis=0, concat_axis=0, tiled=True)
    hidden_local = w_gate_up.shape[2]
    gate_up = w_gate_up[0].reshape(2 * hidden_local, feature_width)
    row_piece = lax.all_gather(arrived[None], "ctx", axis=0, tiled=True)
    piece_count = row_piece.shape[0]
    rows_flat = row_piece.reshape(-1, feature_width)
    both_parts = lax.dot_general(
        rows_flat, gate_up, (((1,), (1,)), ((), ())), preferred_element_type=jnp.float32
    )
    activation = (jax.nn.silu(both_parts[:, :hidden_local]) * both_parts[:, hidden_local:]).astype(
        jnp.bfloat16
    )
    hidden = activation.reshape(piece_count, expert_count, CAP, hidden_local)
    down_cols = w_down[0]
    column_width = down_cols.shape[1]
    hidden_piece = lax.all_gather(hidden, "ctx", axis=3, tiled=True)
    unit_count = hidden_piece.shape[3]
    made_cols = jnp.dot(
        hidden_piece.reshape(-1, unit_count), down_cols, preferred_element_type=jnp.float32
    )
    made_cols = made_cols.astype(jnp.bfloat16).reshape(ctx_count, expert_count, CAP, column_width)
    returned = lax.all_to_all(
        lax.all_to_all(made_cols, "ctx", split_axis=0, concat_axis=3, tiled=True),
        "exp",
        split_axis=1,
        concat_axis=0,
        tiled=True,
    )
    returned = returned.reshape(expert_count * CAP, feature_width)
    picked = lax.dot_general(
        chooser, returned, (((0,), (0,)), ((), ())), preferred_element_type=jnp.float32
    )
    layer_out = (flat_attended + combine[0][:, None] * picked).astype(jnp.bfloat16)
    return layer_out[None]


def solution(mesh):
    placed = (
        P("exp", "ctx", None),
        P("exp", None, "ctx", None),
        P("exp", "ctx"),
        P("exp", "ctx"),
        P("exp", "ctx"),
        P("exp", None, "ctx", None),
        P("exp", None, "ctx"),
    )
    return jax.shard_map(
        shards, mesh=mesh, in_specs=placed, out_specs=P("exp", "ctx", None), check_vma=False
    )
```

profile of v0, /device:TPU:33, one launch (start us, length us, event | category | flops | bytes accessed | tf_op | source)
XLA Modules:
  0.0 687.9 jit_solution(2477227029983482087)
XLA Ops:
  10.8 2.3 copy.43
  14.7 200.1 %while.19 = (s32[]{:T(128)}, f32[2,16,128]{2,1,0:T(8,128)S(1)}, f32[2,16,128]{2,1,0:T(8,128)S(1)}, f32[2,16,128,128]{3,2,1,0:T(8,128)}, bf16[1,2,128,256]{2,3,1,...) while((s32[]{:T(128)}, f32[2,16,128]{2,1,0:T(8,128)S(1)}, ...), condition=%wide.region_3.4_spmd.clone, body=%wide.region_0.3_spmd.clone.sunk | while | flops 276860928 | bytes 29823224 | solution.py:64
  14.7 4.1 collective-permute-start.1
  18.8 1.9 collective-permute-start
  25.4 3.9 collective-permute-start.1
  29.3 1.9 collective-permute-start
  35.8 5.1 collective-permute-start.1
  41.0 1.9 collective-permute-start
  47.5 3.9 collective-permute-start.1
  51.5 1.9 collective-permute-start
  58.0 3.9 collective-permute-start.1
  62.0 1.9 collective-permute-start
  68.5 3.9 collective-permute-start.1
  72.5 1.9 collective-permute-start
  79.1 2.2 collective-permute-done
  81.3 2.4 collective-permute-start.1
  83.8 1.9 collective-permute-start
  90.3 3.7 collective-permute-done.1
  94.0 2.2 collective-permute-done
  96.1 2.4 collective-permute-start.1
  98.6 1.9 collective-permute-start
  105.1 3.7 collective-permute-done.1
  108.8 2.2 collective-permute-done
  111.0 2.4 collective-permute-start.1
  113.4 1.9 collective-permute-start
  119.9 3.7 collective-permute-done.1
  123.6 2.2 collective-permute-done
  125.8 2.4 collective-permute-start.1
  128.3 1.9 collective-permute-start
  134.8 3.7 collective-permute-done.1
  138.5 2.2 collective-permute-done
  140.6 2.4 collective-permute-start.1
  143.1 1.9 collective-permute-start
  149.6 3.7 collective-permute-done.1
  153.3 2.2 collective-permute-done
  155.5 2.4 collective-permute-start.1
  164.4 3.7 collective-permute-done.1
  168.1 2.2 collective-permute-done
  170.3 2.4 collective-permute-start.1
  172.8 1.9 collective-permute-start
  179.2 3.7 collective-permute-done.1
  182.9 2.2 collective-permute-done
  185.1 2.4 collective-permute-start.1
  187.6 1.9 collective-permute-start
  194.1 3.7 collective-permute-done.1
  197.8 2.2 collective-permute-done
  199.9 2.4 collective-permute-start.1
  202.4 1.9 collective-permute-start
  208.9 3.7 collective-permute-done.1
  212.6 2.2 collective-permute-done
  214.8 3.0 copy.48
  222.5 32.7 %all_to_all.32 = bf16[32,2,4096]{2,1,0:T(2,128)(2,1)} all-to-all(bf16[32,2,4096]{2,1,0:T(2,128)(2,1)S(1)} %reshape.55), channel_id=1, replica_groups=mesh['ctx'=16,'exp'=32] {'exp'}, dimensions={0} | all-to-all | bytes 1048576 | tf_op jit(solution)/shard_map/all_to_all | solution.py:86
  255.5 125.6 %all-gather.6.cloned.1.call-done = bf16[512,2,4096]{2,1,0:T(2,128)(2,1)} async-done(((bf16[32,2,4096]{2,1,0:T(2,128)(2,1)}), bf16[512,2,4096]{2,1,0:T(2,128)(2,1)}) %all-gather.6.cloned.1.call-update) | async-done | bytes 8388624 | tf_op jit(solution)/shard_map/all_gather | solution.py:89
  381.1 13.1 %reshape.56 = bf16[1024,4096]{1,0:T(8,128)(2,1)} reshape(bf16[512,2,4096]{2,1,0:T(2,128)(2,1)} %all-gather.6.cloned.1.call-done) | data formatting | bytes 16777216 | tf_op jit(solution)/shard_map/reshape | solution.py:91
  394.2 6.3 fusion.39
  402.2 149.4 %all-gather.4.cloned.1.call-done = bf16[16,32,2,1536]{1,0,2,3:T(8,128)(2,1)} async-done(((bf16[16,32,2,96]{1,0,2,3:T(8,128)(2,1)}), bf16[16,32,2,1536]{1,0,2,3:T(8,128)(2,1)}) %all-gather.4.cloned.1.call-update) | async-done | bytes 3145744 | tf_op jit(solution)/shard_map/all_gather | solution.py:101
  551.6 20.2 %copy.52 = bf16[16,32,2,1536]{3,2,1,0:T(2,128)(2,1)} copy(bf16[16,32,2,1536]{1,0,2,3:T(8,128)(2,1)} %all-gather.4.cloned.1.call-done) | data formatting | bytes 6291456 | tf_op jit(solution)/shard_map/all_gather | solution.py:101
  571.8 7.5 %reshape.58 = bf16[1024,1536]{1,0:T(8,128)(2,1)} reshape(bf16[16,32,2,1536]{3,2,1,0:T(2,128)(2,1)} %copy.52) | data formatting | bytes 6291456 | tf_op jit(solution)/shard_map/reshape | solution.py:104
  579.3 3.1 convolution_convert_fusion.1
  582.7 43.1 %all_to_all.33 = bf16[16,32,2,256]{3,1,2,0:T(8,128)(2,1)S(1)} all-to-all(bf16[16,32,2,256]{3,1,2,0:T(8,128)(2,1)S(1)} %copy.53), channel_id=1, replica_groups=mesh['ctx'=16,'exp'=32] {'ctx'}, dimensions={0} | all-to-all | bytes 1048576 | tf_op jit(solution)/shard_map/all_to_all | solution.py:108
  627.0 14.2 %all-to-all-start.2 = ((bf16[1,32,2,4096]{3,2,0,1:T(2,128)(2,1)}), bf16[1,32,2,4096]{3,2,0,1:T(2,128)(2,1)S(1)}, u32[]{:S(2)}, u32[]{:S(2)}) async-start(bf16[1,32,2,4096]{3,2,0,1:T(2,128)(2,1)} %reshape.68), calls=%async_computation.2 | async-start | bytes 1048576 | tf_op jit(solution)/shard_map/all_to_all | solution.py:107
  641.3 2.9 copy.56
  644.2 33.6 %all-to-all-done.2 = bf16[1,32,2,4096]{3,2,0,1:T(2,128)(2,1)S(1)} async-done(((bf16[1,32,2,4096]{3,2,0,1:T(2,128)(2,1)}), bf16[1,32,2,4096]{3,2,0,1:T(2,128)(2,1)S(1)}, u32[]{:S(2)}, u32[]{:S(2)}) %all-to-all-start.2) | async-done | bytes 524320 | tf_op jit(solution)/shard_map/all_to_all | solution.py:107
  678.0 3.0 fusion.16
  (266 shorter events, 84.0 us)
Async XLA Ops:
  6.5 387.6 %copy-start = (bf16[1,2,96,4096]{3,2,1,0:T(8,128)(2,1)S(1)}, bf16[1,2,96,4096]{3,2,1,0:T(8,128)(2,1)}, u32[]{:S(2)}) copy-start(bf16[1,2,96,4096]{3,2,1,0:T(8,128)(2,1)} %param.14) | copy-start | bytes 4718596
  6.5 374.5 %all-gather.6.cloned.1.call-start = ((), (), s32[]{:S(2)}) async-start(), calls=%async_computation.4 | async-start | bytes 8912896 | tf_op jit(solution)/shard_map/all_gather | solution.py:89
  10.8 3.9 copy-start.6
  14.7 10.6 %collective-permute-start.1 = (s32[1,1,128]{2,1,0:T(1,128)S(1)}, s32[1,1,128]{2,1,0:T(1,128)S(1)}, u32[]{:S(2)}, u32[]{:S(2)}) collective-permute-start(s32[1,1,128]{2,1,0:T(1,128)S(1)} %copy.83), channel_id=1, source_target_pairs={{0,32},{32,64},{64,96},{96,128},{128,160},{160,192},{192,224},{224... | collective-permute-start | bytes 1544 | tf_op jit(solution)/shard_map/while/body/eval_jaxpr/ppermute | solution.py:14
  18.8 6.5 collective-permute-start
  20.9 1.6 copy-start.1
  25.4 10.5 %collective-permute-start.1 = (s32[1,1,128]{2,1,0:T(1,128)S(1)}, s32[1,1,128]{2,1,0:T(1,128)S(1)}, u32[]{:S(2)}, u32[]{:S(2)}) collective-permute-start(s32[1,1,128]{2,1,0:T(1,128)S(1)} %copy.83), channel_id=1, source_target_pairs={{0,32},{32,64},{64,96},{96,128},{128,160},{160,192},{192,224},{224... | collective-permute-start | bytes 1544 | tf_op jit(solution)/shard_map/while/body/eval_jaxpr/ppermute | solution.py:14
  29.3 6.5 collective-permute-start
  31.4 1.6 copy-start.1
  34.5 1.3 copy-start.2
  35.8 11.7 %collective-permute-start.1 = (s32[1,1,128]{2,1,0:T(1,128)S(1)}, s32[1,1,128]{2,1,0:T(1,128)S(1)}, u32[]{:S(2)}, u32[]{:S(2)}) collective-permute-start(s32[1,1,128]{2,1,0:T(1,128)S(1)} %copy.83), channel_id=1, source_target_pairs={{0,32},{32,64},{64,96},{96,128},{128,160},{160,192},{192,224},{224... | collective-permute-start | bytes 1544 | tf_op jit(solution)/shard_map/while/body/eval_jaxpr/ppermute | solution.py:14
  41.0 6.5 collective-permute-start
  43.0 1.6 copy-start.1
  46.2 1.3 copy-start.2
  47.5 10.5 %collective-permute-start.1 = (s32[1,1,128]{2,1,0:T(1,128)S(1)}, s32[1,1,128]{2,1,0:T(1,128)S(1)}, u32[]{:S(2)}, u32[]{:S(2)}) collective-permute-start(s32[1,1,128]{2,1,0:T(1,128)S(1)} %copy.83), channel_id=1, source_target_pairs={{0,32},{32,64},{64,96},{96,128},{128,160},{160,192},{192,224},{224... | collective-permute-start | bytes 1544 | tf_op jit(solution)/shard_map/while/body/eval_jaxpr/ppermute | solution.py:14
  51.5 6.5 collective-permute-start
  53.5 1.6 copy-start.1
  56.6 1.3 copy-start.2
  58.0 10.5 %collective-permute-start.1 = (s32[1,1,128]{2,1,0:T(1,128)S(1)}, s32[1,1,128]{2,1,0:T(1,128)S(1)}, u32[]{:S(2)}, u32[]{:S(2)}) collective-permute-start(s32[1,1,128]{2,1,0:T(1,128)S(1)} %copy.83), channel_id=1, source_target_pairs={{0,32},{32,64},{64,96},{96,128},{128,160},{160,192},{192,224},{224... | collective-permute-start | bytes 1544 | tf_op jit(solution)/shard_map/while/body/eval_jaxpr/ppermute | solution.py:14
  62.0 6.5 collective-permute-start
  64.0 1.6 copy-start.1
  68.5 10.6 %collective-permute-start.1 = (s32[1,1,128]{2,1,0:T(1,128)S(1)}, s32[1,1,128]{2,1,0:T(1,128)S(1)}, u32[]{:S(2)}, u32[]{:S(2)}) collective-permute-start(s32[1,1,128]{2,1,0:T(1,128)S(1)} %copy.83), channel_id=1, source_target_pairs={{0,32},{32,64},{64,96},{96,128},{128,160},{160,192},{192,224},{224... | collective-permute-start | bytes 1544 | tf_op jit(solution)/shard_map/while/body/eval_jaxpr/ppermute | solution.py:14
  72.5 8.9 %collective-permute-start = (bf16[1,2,128,256]{2,3,1,0:T(8,128)(2,1)S(1)}, bf16[1,2,128,256]{2,3,1,0:T(8,128)(2,1)S(1)}, u32[]{:S(2)}, u32[]{:S(2)}) collective-permute-start(bf16[1,2,128,256]{2,3,1,0:T(8,128)(2,1)S(1)} %copy.82), channel_id=1, source_target_pairs={{0,32},{32,64},{64,96},{96,128},{128,160},{160,192},{192,224},{224... | collective-permute-start | bytes 393224 | tf_op jit(solution)/shard_map/while/body/eval_jaxpr/ppermute | solution.py:14
  74.5 1.6 copy-start.1
  77.6 1.3 copy-start.2
  81.3 12.7 %collective-permute-start.1 = (s32[1,1,128]{2,1,0:T(1,128)S(1)}, s32[1,1,128]{2,1,0:T(1,128)S(1)}, u32[]{:S(2)}, u32[]{:S(2)}) collective-permute-start(s32[1,1,128]{2,1,0:T(1,128)S(1)} %copy.83), channel_id=1, source_target_pairs={{0,32},{32,64},{64,96},{96,128},{128,160},{160,192},{192,224},{224... | collective-permute-start | bytes 1544 | tf_op jit(solution)/shard_map/while/body/eval_jaxpr/ppermute | solution.py:14
  83.8 12.4 %collective-permute-start = (bf16[1,2,128,256]{2,3,1,0:T(8,128)(2,1)S(1)}, bf16[1,2,128,256]{2,3,1,0:T(8,128)(2,1)S(1)}, u32[]{:S(2)}, u32[]{:S(2)}) collective-permute-start(bf16[1,2,128,256]{2,3,1,0:T(8,128)(2,1)S(1)} %copy.82), channel_id=1, source_target_pairs={{0,32},{32,64},{64,96},{96,128},{128,160},{160,192},{192,224},{224... | collective-permute-start | bytes 393224 | tf_op jit(solution)/shard_map/while/body/eval_jaxpr/ppermute | solution.py:14
  85.8 1.6 copy-start.1
  88.9 1.3 copy-start.2
  96.1 12.7 %collective-permute-start.1 = (s32[1,1,128]{2,1,0:T(1,128)S(1)}, s32[1,1,128]{2,1,0:T(1,128)S(1)}, u32[]{:S(2)}, u32[]{:S(2)}) collective-permute-start(s32[1,1,128]{2,1,0:T(1,128)S(1)} %copy.83), channel_id=1, source_target_pairs={{0,32},{32,64},{64,96},{96,128},{128,160},{160,192},{192,224},{224... | collective-permute-start | bytes 1544 | tf_op jit(solution)/shard_map/while/body/eval_jaxpr/ppermute | solution.py:14
  98.6 12.4 %collective-permute-start = (bf16[1,2,128,256]{2,3,1,0:T(8,128)(2,1)S(1)}, bf16[1,2,128,256]{2,3,1,0:T(8,128)(2,1)S(1)}, u32[]{:S(2)}, u32[]{:S(2)}) collective-permute-start(bf16[1,2,128,256]{2,3,1,0:T(8,128)(2,1)S(1)} %copy.82), channel_id=1, source_target_pairs={{0,32},{32,64},{64,96},{96,128},{128,160},{160,192},{192,224},{224... | collective-permute-start | bytes 393224 | tf_op jit(solution)/shard_map/while/body/eval_jaxpr/ppermute | solution.py:14
  100.7 1.6 copy-start.1
  103.8 1.3 copy-start.2
  111.0 12.7 %collective-permute-start.1 = (s32[1,1,128]{2,1,0:T(1,128)S(1)}, s32[1,1,128]{2,1,0:T(1,128)S(1)}, u32[]{:S(2)}, u32[]{:S(2)}) collective-permute-start(s32[1,1,128]{2,1,0:T(1,128)S(1)} %copy.83), channel_id=1, source_target_pairs={{0,32},{32,64},{64,96},{96,128},{128,160},{160,192},{192,224},{224... | collective-permute-start | bytes 1544 | tf_op jit(solution)/shard_map/while/body/eval_jaxpr/ppermute | solution.py:14
  113.4 12.4 %collective-permute-start = (bf16[1,2,128,256]{2,3,1,0:T(8,128)(2,1)S(1)}, bf16[1,2,128,256]{2,3,1,0:T(8,128)(2,1)S(1)}, u32[]{:S(2)}, u32[]{:S(2)}) collective-permute-start(bf16[1,2,128,256]{2,3,1,0:T(8,128)(2,1)S(1)} %copy.82), channel_id=1, source_target_pairs={{0,32},{32,64},{64,96},{96,128},{128,160},{160,192},{192,224},{224... | collective-permute-start | bytes 393224 | tf_op jit(solution)/shard_map/while/body/eval_jaxpr/ppermute | solution.py:14
  115.5 1.6 copy-start.1
  118.6 1.3 copy-start.2
  125.8 12.7 %collective-permute-start.1 = (s32[1,1,128]{2,1,0:T(1,128)S(1)}, s32[1,1,128]{2,1,0:T(1,128)S(1)}, u32[]{:S(2)}, u32[]{:S(2)}) collective-permute-start(s32[1,1,128]{2,1,0:T(1,128)S(1)} %copy.83), channel_id=1, source_target_pairs={{0,32},{32,64},{64,96},{96,128},{128,160},{160,192},{192,224},{224... | collective-permute-start | bytes 1544 | tf_op jit(solution)/shard_map/while/body/eval_jaxpr/ppermute | solution.py:14
  128.3 12.4 %collective-permute-start = (bf16[1,2,128,256]{2,3,1,0:T(8,128)(2,1)S(1)}, bf16[1,2,128,256]{2,3,1,0:T(8,128)(2,1)S(1)}, u32[]{:S(2)}, u32[]{:S(2)}) collective-permute-start(bf16[1,2,128,256]{2,3,1,0:T(8,128)(2,1)S(1)} %copy.82), channel_id=1, source_target_pairs={{0,32},{32,64},{64,96},{96,128},{128,160},{160,192},{192,224},{224... | collective-permute-start | bytes 393224 | tf_op jit(solution)/shard_map/while/body/eval_jaxpr/ppermute | solution.py:14
  130.3 1.6 copy-start.1
  133.4 1.3 copy-start.2
  140.6 12.7 %collective-permute-start.1 = (s32[1,1,128]{2,1,0:T(1,128)S(1)}, s32[1,1,128]{2,1,0:T(1,128)S(1)}, u32[]{:S(2)}, u32[]{:S(2)}) collective-permute-start(s32[1,1,128]{2,1,0:T(1,128)S(1)} %copy.83), channel_id=1, source_target_pairs={{0,32},{32,64},{64,96},{96,128},{128,160},{160,192},{192,224},{224... | collective-permute-start | bytes 1544 | tf_op jit(solution)/shard_map/while/body/eval_jaxpr/ppermute | solution.py:14
  143.1 12.4 %collective-permute-start = (bf16[1,2,128,256]{2,3,1,0:T(8,128)(2,1)S(1)}, bf16[1,2,128,256]{2,3,1,0:T(8,128)(2,1)S(1)}, u32[]{:S(2)}, u32[]{:S(2)}) collective-permute-start(bf16[1,2,128,256]{2,3,1,0:T(8,128)(2,1)S(1)} %copy.82), channel_id=1, source_target_pairs={{0,32},{32,64},{64,96},{96,128},{128,160},{160,192},{192,224},{224... | collective-permute-start | bytes 393224 | tf_op jit(solution)/shard_map/while/body/eval_jaxpr/ppermute | solution.py:14
  145.1 1.6 copy-start.1
  155.5 12.7 %collective-permute-start.1 = (s32[1,1,128]{2,1,0:T(1,128)S(1)}, s32[1,1,128]{2,1,0:T(1,128)S(1)}, u32[]{:S(2)}, u32[]{:S(2)}) collective-permute-start(s32[1,1,128]{2,1,0:T(1,128)S(1)} %copy.83), channel_id=1, source_target_pairs={{0,32},{32,64},{64,96},{96,128},{128,160},{160,192},{192,224},{224... | collective-permute-start | bytes 1544 | tf_op jit(solution)/shard_map/while/body/eval_jaxpr/ppermute | solution.py:14
  157.9 12.4 %collective-permute-start = (bf16[1,2,128,256]{2,3,1,0:T(8,128)(2,1)S(1)}, bf16[1,2,128,256]{2,3,1,0:T(8,128)(2,1)S(1)}, u32[]{:S(2)}, u32[]{:S(2)}) collective-permute-start(bf16[1,2,128,256]{2,3,1,0:T(8,128)(2,1)S(1)} %copy.82), channel_id=1, source_target_pairs={{0,32},{32,64},{64,96},{96,128},{128,160},{160,192},{192,224},{224... | collective-permute-start | bytes 393224 | tf_op jit(solution)/shard_map/while/body/eval_jaxpr/ppermute | solution.py:14
  160.0 1.6 copy-start.1
  163.1 1.3 copy-start.2
  170.3 12.7 %collective-permute-start.1 = (s32[1,1,128]{2,1,0:T(1,128)S(1)}, s32[1,1,128]{2,1,0:T(1,128)S(1)}, u32[]{:S(2)}, u32[]{:S(2)}) collective-permute-start(s32[1,1,128]{2,1,0:T(1,128)S(1)} %copy.83), channel_id=1, source_target_pairs={{0,32},{32,64},{64,96},{96,128},{128,160},{160,192},{192,224},{224... | collective-permute-start | bytes 1544 | tf_op jit(solution)/shard_map/while/body/eval_jaxpr/ppermute | solution.py:14
  172.8 12.4 %collective-permute-start = (bf16[1,2,128,256]{2,3,1,0:T(8,128)(2,1)S(1)}, bf16[1,2,128,256]{2,3,1,0:T(8,128)(2,1)S(1)}, u32[]{:S(2)}, u32[]{:S(2)}) collective-permute-start(bf16[1,2,128,256]{2,3,1,0:T(8,128)(2,1)S(1)} %copy.82), channel_id=1, source_target_pairs={{0,32},{32,64},{64,96},{96,128},{128,160},{160,192},{192,224},{224... | collective-permute-start | bytes 393224 | tf_op jit(solution)/shard_map/while/body/eval_jaxpr/ppermute | solution.py:14
  174.8 1.6 copy-start.1
  177.9 1.3 copy-start.2
  185.1 12.7 %collective-permute-start.1 = (s32[1,1,128]{2,1,0:T(1,128)S(1)}, s32[1,1,128]{2,1,0:T(1,128)S(1)}, u32[]{:S(2)}, u32[]{:S(2)}) collective-permute-start(s32[1,1,128]{2,1,0:T(1,128)S(1)} %copy.83), channel_id=1, source_target_pairs={{0,32},{32,64},{64,96},{96,128},{128,160},{160,192},{192,224},{224... | collective-permute-start | bytes 1544 | tf_op jit(solution)/shard_map/while/body/eval_jaxpr/ppermute | solution.py:14
  187.6 12.4 %collective-permute-start = (bf16[1,2,128,256]{2,3,1,0:T(8,128)(2,1)S(1)}, bf16[1,2,128,256]{2,3,1,0:T(8,128)(2,1)S(1)}, u32[]{:S(2)}, u32[]{:S(2)}) collective-permute-start(bf16[1,2,128,256]{2,3,1,0:T(8,128)(2,1)S(1)} %copy.82), channel_id=1, source_target_pairs={{0,32},{32,64},{64,96},{96,128},{128,160},{160,192},{192,224},{224... | collective-permute-start | bytes 393224 | tf_op jit(solution)/shard_map/while/body/eval_jaxpr/ppermute | solution.py:14
  189.6 1.6 copy-start.1
  199.9 12.7 %collective-permute-start.1 = (s32[1,1,128]{2,1,0:T(1,128)S(1)}, s32[1,1,128]{2,1,0:T(1,128)S(1)}, u32[]{:S(2)}, u32[]{:S(2)}) collective-permute-start(s32[1,1,128]{2,1,0:T(1,128)S(1)} %copy.83), channel_id=1, source_target_pairs={{0,32},{32,64},{64,96},{96,128},{128,160},{160,192},{192,224},{224... | collective-permute-start | bytes 1544 | tf_op jit(solution)/shard_map/while/body/eval_jaxpr/ppermute | solution.py:14
  202.4 12.4 %collective-permute-start = (bf16[1,2,128,256]{2,3,1,0:T(8,128)(2,1)S(1)}, bf16[1,2,128,256]{2,3,1,0:T(8,128)(2,1)S(1)}, u32[]{:S(2)}, u32[]{:S(2)}) collective-permute-start(bf16[1,2,128,256]{2,3,1,0:T(8,128)(2,1)S(1)} %copy.82), channel_id=1, source_target_pairs={{0,32},{32,64},{64,96},{96,128},{128,160},{160,192},{192,224},{224... | collective-permute-start | bytes 393224 | tf_op jit(solution)/shard_map/while/body/eval_jaxpr/ppermute | solution.py:14
  204.5 1.6 copy-start.1
  214.8 3.1 copy-start.3
  217.9 1.6 copy-start.5
  220.3 1.3 copy-start.4
  255.3 296.3 %all-gather.4.cloned.1.call-start = ((), (), s32[]{:S(2)}) async-start(), calls=%async_computation.3 | async-start | bytes 13369344 | tf_op jit(solution)/shard_map/all_gather | solution.py:101
  627.0 50.7 %all-to-all-start.2 = ((bf16[1,32,2,4096]{3,2,0,1:T(2,128)(2,1)}), bf16[1,32,2,4096]{3,2,0,1:T(2,128)(2,1)S(1)}, u32[]{:S(2)}, u32[]{:S(2)}) async-start(bf16[1,32,2,4096]{3,2,0,1:T(2,128)(2,1)} %reshape.68), calls=%async_computation.2 | async-start | bytes 1048576 | tf_op jit(solution)/shard_map/all_to_all | solution.py:107
  641.3 36.7 %copy-start.7 = (f32[1,128]{1,0:T(1,128)S(1)}, f32[1,128]{1,0:T(1,128)}, u32[]{:S(2)}) copy-start(f32[1,128]{1,0:T(1,128)} %param.13) | copy-start | bytes 1540
  (5 other events, 6.7 us)
Sparse Core Ops, SparseCore 0:
  255.4 125.6 all-gather.5
  402.3 149.2 all-gather.3
where the time goes:
time: 691 us; the launch traced here: 688 us
  waiting for transfers between devices  364 us (53%)
  starting transfers between devices  90.1 us (13%)
  local copies, waits for them, and re-layouts  85.2 us (12%)
  blocking collectives  75.9 us (11%)
  matrix products  44.7 us (6%)
  between operations  13.6 us (2%)
  other arithmetic  13.1 us (2%)
    all_gather x1, waiting for transfers between devices, shards(): hidden_piece = lax.all_gather(hidden, 'ctx', axis=3, tiled=True)  149 us
    all_gather x1, waiting for transfers between devices, shards(): row_piece = lax.all_gather(arrived[None], 'ctx', axis=0, tiled=True)  126 us
    ppermute x30, starting transfers between devices, shifted(): lax.ppermute(value, axis, [(i, (i + by) % length) for i in range(length)])  75.7 us
    ppermute x30, waiting for transfers between devices, shifted(): lax.ppermute(value, axis, [(i, (i + by) % length) for i in range(length)])  55.2 us
    all_to_all x1, blocking collectives, shards(): lax.all_to_all(made_cols, 'ctx', split_axis=0, concat_axis=3, tiled=True)  43.1 us
    all_to_all x1, waiting for transfers between devices, shards(): lax.all_to_all(lax.all_to_all(made_cols, 'ctx', split_axis=0, concat_axis...  33.6 us
    all_to_all x1, blocking collectives, shards(): lax.all_to_all(outgoing, 'exp', split_axis=0, concat_axis=0, tiled=True)  32.7 us
    while x105, local copies, waits for them, and re-layouts  27.2 us
  transfers between devices with their start and end apart: 33, of which 23 were waited for; matrix products, arithmetic and copies ran while one was open for 6% of the time, Pallas kernels for 0%

commit v1 on v0

--- a/solution.py
+++ b/solution.py
@@ -86,7 +86,13 @@
     arrived = lax.all_to_all(outgoing, "exp", split_axis=0, concat_axis=0, tiled=True)
     hidden_local = w_gate_up.shape[2]
     gate_up = w_gate_up[0].reshape(2 * hidden_local, feature_width)
-    row_piece = lax.all_gather(arrived[None], "ctx", axis=0, tiled=True)
+
+    def fix_bands_by_axis(u_in):
+        return jnp.concatenate(
+            lax.all_to_all(jnp.stack(lax.axis_size("ctx") * [u_in]), "ctx", 0, 0), 0
+        )
+
+    row_piece = fix_bands_by_axis(arrived[None])
     piece_count = row_piece.shape[0]
     rows_flat = row_piece.reshape(-1, feature_width)
     both_parts = lax.dot_general(

time: 691 us -> 955 us (1.38)
  blocking collectives: 75.9 us -> 475 us
  waiting for transfers between devices: 364 us -> 222 us
    all_to_all x0 -> x1, blocking collectives: none -> 399 us  [fix_bands_by_axis(): lax.all_to_all(jnp.stack(lax.axis_size('ctx') * [u_in]), 'ctx', 0, 0)]
    all_gather x1 -> x0, waiting for transfers between devices: 126 us -> none  [shards(): row_piece = lax.all_gather(arrived[None], 'ctx', axis=0, tiled=True)]
    another operation x0 -> x2, local copies, waits for them, and re-layouts: none -> 20.8 us  [the longest x1 13.1 us: shards(): rows_flat = row_piece.reshape(-1, feature_width)]
    all_gather x1, waiting for transfers between devices: 149 us -> 133 us  [shards(): hidden_piece = lax.all_gather(hidden, 'ctx', axis=3, tiled=True)]
    reshape x1 -> x0, local copies, waits for them, and re-layouts: 13.1 us -> none  [shards(): rows_flat = row_piece.reshape(-1, feature_width)]
  transfers between devices with their start and end apart: 33 -> 32, of which waited for: 23 -> 22; matrix products, arithmetic and copies ran while one was open for 6% -> 5% of each run, Pallas kernels for 0% -> 0%
where the time goes in v1:
time: 955 us; the launch traced here: 952 us
  blocking collectives  475 us (50%)
  waiting for transfers between devices  222 us (23%)
  local copies, waits for them, and re-layouts  92.8 us (10%)
  starting transfers between devices  89.7 us (9%)
  matrix products  44.7 us (5%)
  between operations  13.6 us (1%)
  other arithmetic  13.1 us (1%)
    all_to_all x1, blocking collectives, fix_bands_by_axis(): lax.all_to_all(jnp.stack(lax.axis_size('ctx') * [u_in]), 'ctx', 0, 0)  399 us
    all_gather x1, waiting for transfers between devices, shards(): hidden_piece = lax.all_gather(hidden, 'ctx', axis=3, tiled=True)  133 us
    ppermute x30, starting transfers between devices, shifted(): lax.ppermute(value, axis, [(i, (i + by) % length) for i in range(length)])  75.5 us
    ppermute x30, waiting for transfers between devices, shifted(): lax.ppermute(value, axis, [(i, (i + by) % length) for i in range(length)])  55.4 us
    all_to_all x1, blocking collectives, shards(): lax.all_to_all(made_cols, 'ctx', split_axis=0, concat_axis=3, tiled=True)  43.1 us
    all_to_all x1, waiting for transfers between devices, shards(): lax.all_to_all(lax.all_to_all(made_cols, 'ctx', split_axis=0, concat_axis...  33.5 us
    all_to_all x1, blocking collectives, shards(): lax.all_to_all(outgoing, 'exp', split_axis=0, concat_axis=0, tiled=True)  32.6 us
    while x105, local copies, waits for them, and re-layouts  27.1 us
  transfers between devices with their start and end apart: 32, of which 22 were waited for; matrix products, arithmetic and copies ran while one was open for 5% of the time, Pallas kernels for 0%

profile of v1, /device:TPU:33, one launch (start us, length us, event | category | flops | bytes accessed | tf_op | source)
XLA Modules:
  0.0 952.3 jit_solution(413220307102580017)
XLA Ops:
  10.8 2.3 copy.43
  14.7 200.1 %while.19 = (s32[]{:T(128)}, f32[2,16,128]{2,1,0:T(8,128)S(1)}, f32[2,16,128]{2,1,0:T(8,128)S(1)}, f32[2,16,128,128]{3,2,1,0:T(8,128)}, bf16[1,2,128,256]{2,3,1,...) while((s32[]{:T(128)}, f32[2,16,128]{2,1,0:T(8,128)S(1)}, ...), condition=%wide.region_3.4_spmd.clone, body=%wide.region_0.3_spmd.clone.sunk | while | flops 276860928 | bytes 29823224 | solution.py:64
  14.7 4.1 collective-permute-start.1
  18.8 1.9 collective-permute-start
  25.3 3.9 collective-permute-start.1
  29.3 1.9 collective-permute-start
  35.8 5.1 collective-permute-start.1
  41.0 1.9 collective-permute-start
  47.5 3.9 collective-permute-start.1
  51.5 1.9 collective-permute-start
  58.0 3.9 collective-permute-start.1
  62.0 1.9 collective-permute-start
  68.5 3.9 collective-permute-start.1
  72.4 1.9 collective-permute-start
  79.1 2.2 collective-permute-done
  81.3 2.4 collective-permute-start.1
  83.8 1.9 collective-permute-start
  90.3 3.7 collective-permute-done.1
  94.0 2.2 collective-permute-done
  96.1 2.4 collective-permute-start.1
  98.6 1.9 collective-permute-start
  105.1 3.7 collective-permute-done.1
  108.8 2.2 collective-permute-done
  111.0 2.4 collective-permute-start.1
  113.4 1.9 collective-permute-start
  119.9 3.7 collective-permute-done.1
  123.6 2.2 collective-permute-done
  125.8 2.4 collective-permute-start.1
  128.2 1.9 collective-permute-start
  134.7 3.7 collective-permute-done.1
  138.5 2.2 collective-permute-done
  140.6 2.4 collective-permute-start.1
  143.1 1.9 collective-permute-start
  149.6 3.7 collective-permute-done.1
  153.3 2.2 collective-permute-done
  155.5 2.4 collective-permute-start.1
  164.4 3.7 collective-permute-done.1
  168.1 2.2 collective-permute-done
  170.3 2.4 collective-permute-start.1
  172.7 1.9 collective-permute-start
  179.2 3.7 collective-permute-done.1
  182.9 2.2 collective-permute-done
  185.1 2.4 collective-permute-start.1
  187.6 1.9 collective-permute-start
  194.1 3.7 collective-permute-done.1
  197.8 2.2 collective-permute-done
  199.9 2.4 collective-permute-start.1
  208.9 3.7 collective-permute-done.1
  212.6 2.2 collective-permute-done
  214.8 3.0 copy.48
  222.5 32.6 %all_to_all.37 = bf16[32,2,4096]{2,1,0:T(2,128)(2,1)S(1)} all-to-all(bf16[32,2,4096]{2,1,0:T(2,128)(2,1)S(1)} %reshape.54), channel_id=1, replica_groups=mesh['ctx'=16,'exp'=32] {'exp'}, dimensions={0} | all-to-all | bytes 1048576 | tf_op jit(solution)/shard_map/all_to_all | solution.py:86
  255.1 7.7 stack.3
  262.8 399.5 %all_to_all.38 = bf16[16,1,32,2,4096]{4,3,2,1,0:T(2,128)(2,1)} all-to-all(bf16[16,1,32,2,4096]{4,3,2,1,0:T(2,128)(2,1)S(1)} %stack.3), channel_id=1, replica_groups=mesh['ctx'=16,'exp'=32] {'ctx'}, dimensions={0} | all-to-all | bytes 16777216 | tf_op jit(solution)/shard_map/all_to_all | solution.py:92
  662.3 13.1 %reshape_reshape.3 = bf16[1024,4096]{1,0:T(8,128)(2,1)} reshape(bf16[16,1,32,2,4096]{4,3,2,1,0:T(2,128)(2,1)} %all_to_all.38) | data formatting | bytes 16777216 | tf_op jit(solution)/shard_map/reshape;reshape | solution.py:97
  675.4 6.3 fusion.39
  683.5 132.6 %all-gather.2.cloned.1.call-done = bf16[16,32,2,1536]{1,0,2,3:T(8,128)(2,1)} async-done(((bf16[16,32,2,96]{1,0,2,3:T(8,128)(2,1)}), bf16[16,32,2,1536]{1,0,2,3:T(8,128)(2,1)}) %all-gather.2.cloned.1.call-update) | async-done | bytes 3145744 | tf_op jit(solution)/shard_map/all_gather | solution.py:107
  816.1 20.2 %copy.52 = bf16[16,32,2,1536]{3,2,1,0:T(2,128)(2,1)} copy(bf16[16,32,2,1536]{1,0,2,3:T(8,128)(2,1)} %all-gather.2.cloned.1.call-done) | data formatting | bytes 6291456 | tf_op jit(solution)/shard_map/all_gather | solution.py:107
  836.3 7.5 reshape.56
  843.8 3.1 convolution_convert_fusion.1
  847.2 43.1 %all_to_all.39 = bf16[16,32,2,256]{3,1,2,0:T(8,128)(2,1)S(1)} all-to-all(bf16[16,32,2,256]{3,1,2,0:T(8,128)(2,1)S(1)} %copy.53), channel_id=1, replica_groups=mesh['ctx'=16,'exp'=32] {'ctx'}, dimensions={0} | all-to-all | bytes 1048576 | tf_op jit(solution)/shard_map/all_to_all | solution.py:114
  891.5 14.2 %all-to-all-start.3 = ((bf16[1,32,2,4096]{3,2,0,1:T(2,128)(2,1)}), bf16[1,32,2,4096]{3,2,0,1:T(2,128)(2,1)S(1)}, u32[]{:S(2)}, u32[]{:S(2)}) async-start(bf16[1,32,2,4096]{3,2,0,1:T(2,128)(2,1)} %reshape.64), calls=%async_computation.3 | async-start | bytes 1048576 | tf_op jit(solution)/shard_map/all_to_all | solution.py:113
  905.8 2.9 copy.56
  908.7 33.5 %all-to-all-done.3 = bf16[1,32,2,4096]{3,2,0,1:T(2,128)(2,1)S(1)} async-done(((bf16[1,32,2,4096]{3,2,0,1:T(2,128)(2,1)}), bf16[1,32,2,4096]{3,2,0,1:T(2,128)(2,1)S(1)}, u32[]{:S(2)}, u32[]{:S(2)}) %all-to-all-start.3) | async-done | bytes 524320 | tf_op jit(solution)/shard_map/all_to_all | solution.py:113
  942.4 3.0 fusion.16
  (265 shorter events, 85.6 us)
Async XLA Ops:
  6.5 668.9 %copy-start = (bf16[1,2,96,4096]{3,2,1,0:T(8,128)(2,1)S(1)}, bf16[1,2,96,4096]{3,2,1,0:T(8,128)(2,1)}, u32[]{:S(2)}) copy-start(bf16[1,2,96,4096]{3,2,1,0:T(8,128)(2,1)} %param.14) | copy-start | bytes 4718596
  6.5 809.6 %all-gather.2.cloned.1.call-start = ((), (), s32[]{:S(2)}) async-start(), calls=%async_computation.4 | async-start | bytes 13369344 | tf_op jit(solution)/shard_map/all_gather | solution.py:107
  10.8 3.9 copy-start.6
  14.7 10.6 %collective-permute-start.1 = (s32[1,1,128]{2,1,0:T(1,128)S(1)}, s32[1,1,128]{2,1,0:T(1,128)S(1)}, u32[]{:S(2)}, u32[]{:S(2)}) collective-permute-start(s32[1,1,128]{2,1,0:T(1,128)S(1)} %copy.83), channel_id=1, source_target_pairs={{0,32},{32,64},{64,96},{96,128},{128,160},{160,192},{192,224},{224... | collective-permute-start | bytes 1544 | tf_op jit(solution)/shard_map/while/body/eval_jaxpr/ppermute | solution.py:14
  18.8 6.5 collective-permute-start
  20.9 1.6 copy-start.1
  24.0 1.3 copy-start.2
  25.3 10.5 %collective-permute-start.1 = (s32[1,1,128]{2,1,0:T(1,128)S(1)}, s32[1,1,128]{2,1,0:T(1,128)S(1)}, u32[]{:S(2)}, u32[]{:S(2)}) collective-permute-start(s32[1,1,128]{2,1,0:T(1,128)S(1)} %copy.83), channel_id=1, source_target_pairs={{0,32},{32,64},{64,96},{96,128},{128,160},{160,192},{192,224},{224... | collective-permute-start | bytes 1544 | tf_op jit(solution)/shard_map/while/body/eval_jaxpr/ppermute | solution.py:14
  29.3 6.5 collective-permute-start
  31.3 1.6 copy-start.1
  34.5 1.3 copy-start.2
  35.8 11.7 %collective-permute-start.1 = (s32[1,1,128]{2,1,0:T(1,128)S(1)}, s32[1,1,128]{2,1,0:T(1,128)S(1)}, u32[]{:S(2)}, u32[]{:S(2)}) collective-permute-start(s32[1,1,128]{2,1,0:T(1,128)S(1)} %copy.83), channel_id=1, source_target_pairs={{0,32},{32,64},{64,96},{96,128},{128,160},{160,192},{192,224},{224... | collective-permute-start | bytes 1544 | tf_op jit(solution)/shard_map/while/body/eval_jaxpr/ppermute | solution.py:14
  41.0 6.5 collective-permute-start
  43.0 1.6 copy-start.1
  46.1 1.3 copy-start.2
  47.5 10.5 %collective-permute-start.1 = (s32[1,1,128]{2,1,0:T(1,128)S(1)}, s32[1,1,128]{2,1,0:T(1,128)S(1)}, u32[]{:S(2)}, u32[]{:S(2)}) collective-permute-start(s32[1,1,128]{2,1,0:T(1,128)S(1)} %copy.83), channel_id=1, source_target_pairs={{0,32},{32,64},{64,96},{96,128},{128,160},{160,192},{192,224},{224... | collective-permute-start | bytes 1544 | tf_op jit(solution)/shard_map/while/body/eval_jaxpr/ppermute | solution.py:14
  51.5 6.5 collective-permute-start
  53.5 1.6 copy-start.1
  56.6 1.3 copy-start.2
  58.0 10.5 %collective-permute-start.1 = (s32[1,1,128]{2,1,0:T(1,128)S(1)}, s32[1,1,128]{2,1,0:T(1,128)S(1)}, u32[]{:S(2)}, u32[]{:S(2)}) collective-permute-start(s32[1,1,128]{2,1,0:T(1,128)S(1)} %copy.83), channel_id=1, source_target_pairs={{0,32},{32,64},{64,96},{96,128},{128,160},{160,192},{192,224},{224... | collective-permute-start | bytes 1544 | tf_op jit(solution)/shard_map/while/body/eval_jaxpr/ppermute | solution.py:14
  62.0 6.5 collective-permute-start
  64.0 1.6 copy-start.1
  67.1 1.3 copy-start.2
  68.5 10.7 %collective-permute-start.1 = (s32[1,1,128]{2,1,0:T(1,128)S(1)}, s32[1,1,128]{2,1,0:T(1,128)S(1)}, u32[]{:S(2)}, u32[]{:S(2)}) collective-permute-start(s32[1,1,128]{2,1,0:T(1,128)S(1)} %copy.83), channel_id=1, source_target_pairs={{0,32},{32,64},{64,96},{96,128},{128,160},{160,192},{192,224},{224... | collective-permute-start | bytes 1544 | tf_op jit(solution)/shard_map/while/body/eval_jaxpr/ppermute | solution.py:14
  72.4 8.9 collective-permute-start
  74.5 1.6 copy-start.1
  77.6 1.3 copy-start.2
  81.3 12.7 %collective-permute-start.1 = (s32[1,1,128]{2,1,0:T(1,128)S(1)}, s32[1,1,128]{2,1,0:T(1,128)S(1)}, u32[]{:S(2)}, u32[]{:S(2)}) collective-permute-start(s32[1,1,128]{2,1,0:T(1,128)S(1)} %copy.83), channel_id=1, source_target_pairs={{0,32},{32,64},{64,96},{96,128},{128,160},{160,192},{192,224},{224... | collective-permute-start | bytes 1544 | tf_op jit(solution)/shard_map/while/body/eval_jaxpr/ppermute | solution.py:14
  83.8 12.4 %collective-permute-start = (bf16[1,2,128,256]{2,3,1,0:T(8,128)(2,1)S(1)}, bf16[1,2,128,256]{2,3,1,0:T(8,128)(2,1)S(1)}, u32[]{:S(2)}, u32[]{:S(2)}) collective-permute-start(bf16[1,2,128,256]{2,3,1,0:T(8,128)(2,1)S(1)} %copy.82), channel_id=1, source_target_pairs={{0,32},{32,64},{64,96},{96,128},{128,160},{160,192},{192,224},{224... | collective-permute-start | bytes 393224 | tf_op jit(solution)/shard_map/while/body/eval_jaxpr/ppermute | solution.py:14
  85.8 1.6 copy-start.1
  88.9 1.3 copy-start.2
  96.1 12.7 %collective-permute-start.1 = (s32[1,1,128]{2,1,0:T(1,128)S(1)}, s32[1,1,128]{2,1,0:T(1,128)S(1)}, u32[]{:S(2)}, u32[]{:S(2)}) collective-permute-start(s32[1,1,128]{2,1,0:T(1,128)S(1)} %copy.83), channel_id=1, source_target_pairs={{0,32},{32,64},{64,96},{96,128},{128,160},{160,192},{192,224},{224... | collective-permute-start | bytes 1544 | tf_op jit(solution)/shard_map/while/body/eval_jaxpr/ppermute | solution.py:14
  98.6 12.4 %collective-permute-start = (bf16[1,2,128,256]{2,3,1,0:T(8,128)(2,1)S(1)}, bf16[1,2,128,256]{2,3,1,0:T(8,128)(2,1)S(1)}, u32[]{:S(2)}, u32[]{:S(2)}) collective-permute-start(bf16[1,2,128,256]{2,3,1,0:T(8,128)(2,1)S(1)} %copy.82), channel_id=1, source_target_pairs={{0,32},{32,64},{64,96},{96,128},{128,160},{160,192},{192,224},{224... | collective-permute-start | bytes 393224 | tf_op jit(solution)/shard_map/while/body/eval_jaxpr/ppermute | solution.py:14
  100.6 1.6 copy-start.1
  103.7 1.3 copy-start.2
  111.0 12.7 %collective-permute-start.1 = (s32[1,1,128]{2,1,0:T(1,128)S(1)}, s32[1,1,128]{2,1,0:T(1,128)S(1)}, u32[]{:S(2)}, u32[]{:S(2)}) collective-permute-start(s32[1,1,128]{2,1,0:T(1,128)S(1)} %copy.83), channel_id=1, source_target_pairs={{0,32},{32,64},{64,96},{96,128},{128,160},{160,192},{192,224},{224... | collective-permute-start | bytes 1544 | tf_op jit(solution)/shard_map/while/body/eval_jaxpr/ppermute | solution.py:14
  113.4 12.4 %collective-permute-start = (bf16[1,2,128,256]{2,3,1,0:T(8,128)(2,1)S(1)}, bf16[1,2,128,256]{2,3,1,0:T(8,128)(2,1)S(1)}, u32[]{:S(2)}, u32[]{:S(2)}) collective-permute-start(bf16[1,2,128,256]{2,3,1,0:T(8,128)(2,1)S(1)} %copy.82), channel_id=1, source_target_pairs={{0,32},{32,64},{64,96},{96,128},{128,160},{160,192},{192,224},{224... | collective-permute-start | bytes 393224 | tf_op jit(solution)/shard_map/while/body/eval_jaxpr/ppermute | solution.py:14
  115.5 1.6 copy-start.1
  118.6 1.3 copy-start.2
  125.8 12.7 %collective-permute-start.1 = (s32[1,1,128]{2,1,0:T(1,128)S(1)}, s32[1,1,128]{2,1,0:T(1,128)S(1)}, u32[]{:S(2)}, u32[]{:S(2)}) collective-permute-start(s32[1,1,128]{2,1,0:T(1,128)S(1)} %copy.83), channel_id=1, source_target_pairs={{0,32},{32,64},{64,96},{96,128},{128,160},{160,192},{192,224},{224... | collective-permute-start | bytes 1544 | tf_op jit(solution)/shard_map/while/body/eval_jaxpr/ppermute | solution.py:14
  128.2 12.4 %collective-permute-start = (bf16[1,2,128,256]{2,3,1,0:T(8,128)(2,1)S(1)}, bf16[1,2,128,256]{2,3,1,0:T(8,128)(2,1)S(1)}, u32[]{:S(2)}, u32[]{:S(2)}) collective-permute-start(bf16[1,2,128,256]{2,3,1,0:T(8,128)(2,1)S(1)} %copy.82), channel_id=1, source_target_pairs={{0,32},{32,64},{64,96},{96,128},{128,160},{160,192},{192,224},{224... | collective-permute-start | bytes 393224 | tf_op jit(solution)/shard_map/while/body/eval_jaxpr/ppermute | solution.py:14
  130.3 1.6 copy-start.1
  133.4 1.3 copy-start.2
  140.6 12.7 %collective-permute-start.1 = (s32[1,1,128]{2,1,0:T(1,128)S(1)}, s32[1,1,128]{2,1,0:T(1,128)S(1)}, u32[]{:S(2)}, u32[]{:S(2)}) collective-permute-start(s32[1,1,128]{2,1,0:T(1,128)S(1)} %copy.83), channel_id=1, source_target_pairs={{0,32},{32,64},{64,96},{96,128},{128,160},{160,192},{192,224},{224... | collective-permute-start | bytes 1544 | tf_op jit(solution)/shard_map/while/body/eval_jaxpr/ppermute | solution.py:14
  143.1 12.4 %collective-permute-start = (bf16[1,2,128,256]{2,3,1,0:T(8,128)(2,1)S(1)}, bf16[1,2,128,256]{2,3,1,0:T(8,128)(2,1)S(1)}, u32[]{:S(2)}, u32[]{:S(2)}) collective-permute-start(bf16[1,2,128,256]{2,3,1,0:T(8,128)(2,1)S(1)} %copy.82), channel_id=1, source_target_pairs={{0,32},{32,64},{64,96},{96,128},{128,160},{160,192},{192,224},{224... | collective-permute-start | bytes 393224 | tf_op jit(solution)/shard_map/while/body/eval_jaxpr/ppermute | solution.py:14
  145.1 1.6 copy-start.1
  155.5 12.7 %collective-permute-start.1 = (s32[1,1,128]{2,1,0:T(1,128)S(1)}, s32[1,1,128]{2,1,0:T(1,128)S(1)}, u32[]{:S(2)}, u32[]{:S(2)}) collective-permute-start(s32[1,1,128]{2,1,0:T(1,128)S(1)} %copy.83), channel_id=1, source_target_pairs={{0,32},{32,64},{64,96},{96,128},{128,160},{160,192},{192,224},{224... | collective-permute-start | bytes 1544 | tf_op jit(solution)/shard_map/while/body/eval_jaxpr/ppermute | solution.py:14
  157.9 12.4 %collective-permute-start = (bf16[1,2,128,256]{2,3,1,0:T(8,128)(2,1)S(1)}, bf16[1,2,128,256]{2,3,1,0:T(8,128)(2,1)S(1)}, u32[]{:S(2)}, u32[]{:S(2)}) collective-permute-start(bf16[1,2,128,256]{2,3,1,0:T(8,128)(2,1)S(1)} %copy.82), channel_id=1, source_target_pairs={{0,32},{32,64},{64,96},{96,128},{128,160},{160,192},{192,224},{224... | collective-permute-start | bytes 393224 | tf_op jit(solution)/shard_map/while/body/eval_jaxpr/ppermute | solution.py:14
  159.9 1.6 copy-start.1
  170.3 12.7 %collective-permute-start.1 = (s32[1,1,128]{2,1,0:T(1,128)S(1)}, s32[1,1,128]{2,1,0:T(1,128)S(1)}, u32[]{:S(2)}, u32[]{:S(2)}) collective-permute-start(s32[1,1,128]{2,1,0:T(1,128)S(1)} %copy.83), channel_id=1, source_target_pairs={{0,32},{32,64},{64,96},{96,128},{128,160},{160,192},{192,224},{224... | collective-permute-start | bytes 1544 | tf_op jit(solution)/shard_map/while/body/eval_jaxpr/ppermute | solution.py:14
  172.7 12.4 %collective-permute-start = (bf16[1,2,128,256]{2,3,1,0:T(8,128)(2,1)S(1)}, bf16[1,2,128,256]{2,3,1,0:T(8,128)(2,1)S(1)}, u32[]{:S(2)}, u32[]{:S(2)}) collective-permute-start(bf16[1,2,128,256]{2,3,1,0:T(8,128)(2,1)S(1)} %copy.82), channel_id=1, source_target_pairs={{0,32},{32,64},{64,96},{96,128},{128,160},{160,192},{192,224},{224... | collective-permute-start | bytes 393224 | tf_op jit(solution)/shard_map/while/body/eval_jaxpr/ppermute | solution.py:14
  174.8 1.6 copy-start.1
  185.1 12.7 %collective-permute-start.1 = (s32[1,1,128]{2,1,0:T(1,128)S(1)}, s32[1,1,128]{2,1,0:T(1,128)S(1)}, u32[]{:S(2)}, u32[]{:S(2)}) collective-permute-start(s32[1,1,128]{2,1,0:T(1,128)S(1)} %copy.83), channel_id=1, source_target_pairs={{0,32},{32,64},{64,96},{96,128},{128,160},{160,192},{192,224},{224... | collective-permute-start | bytes 1544 | tf_op jit(solution)/shard_map/while/body/eval_jaxpr/ppermute | solution.py:14
  187.6 12.4 %collective-permute-start = (bf16[1,2,128,256]{2,3,1,0:T(8,128)(2,1)S(1)}, bf16[1,2,128,256]{2,3,1,0:T(8,128)(2,1)S(1)}, u32[]{:S(2)}, u32[]{:S(2)}) collective-permute-start(bf16[1,2,128,256]{2,3,1,0:T(8,128)(2,1)S(1)} %copy.82), channel_id=1, source_target_pairs={{0,32},{32,64},{64,96},{96,128},{128,160},{160,192},{192,224},{224... | collective-permute-start | bytes 393224 | tf_op jit(solution)/shard_map/while/body/eval_jaxpr/ppermute | solution.py:14
  189.6 1.6 copy-start.1
  192.7 1.3 copy-start.2
  199.9 12.7 %collective-permute-start.1 = (s32[1,1,128]{2,1,0:T(1,128)S(1)}, s32[1,1,128]{2,1,0:T(1,128)S(1)}, u32[]{:S(2)}, u32[]{:S(2)}) collective-permute-start(s32[1,1,128]{2,1,0:T(1,128)S(1)} %copy.83), channel_id=1, source_target_pairs={{0,32},{32,64},{64,96},{96,128},{128,160},{160,192},{192,224},{224... | collective-permute-start | bytes 1544 | tf_op jit(solution)/shard_map/while/body/eval_jaxpr/ppermute | solution.py:14
  202.4 12.4 %collective-permute-start = (bf16[1,2,128,256]{2,3,1,0:T(8,128)(2,1)S(1)}, bf16[1,2,128,256]{2,3,1,0:T(8,128)(2,1)S(1)}, u32[]{:S(2)}, u32[]{:S(2)}) collective-permute-start(bf16[1,2,128,256]{2,3,1,0:T(8,128)(2,1)S(1)} %copy.82), channel_id=1, source_target_pairs={{0,32},{32,64},{64,96},{96,128},{128,160},{160,192},{192,224},{224... | collective-permute-start | bytes 393224 | tf_op jit(solution)/shard_map/while/body/eval_jaxpr/ppermute | solution.py:14
  204.4 1.6 copy-start.1
  214.8 3.1 copy-start.3
  217.9 1.6 copy-start.5
  220.3 1.3 copy-start.4
  891.5 50.7 %all-to-all-start.3 = ((bf16[1,32,2,4096]{3,2,0,1:T(2,128)(2,1)}), bf16[1,32,2,4096]{3,2,0,1:T(2,128)(2,1)S(1)}, u32[]{:S(2)}, u32[]{:S(2)}) async-start(bf16[1,32,2,4096]{3,2,0,1:T(2,128)(2,1)} %reshape.64), calls=%async_computation.3 | async-start | bytes 1048576 | tf_op jit(solution)/shard_map/all_to_all | solution.py:113
  905.8 36.7 %copy-start.7 = (f32[1,128]{1,0:T(1,128)S(1)}, f32[1,128]{1,0:T(1,128)}, u32[]{:S(2)}) copy-start(f32[1,128]{1,0:T(1,128)} %param.13) | copy-start | bytes 1540
  (4 other events, 5.3 us)
Sparse Core Ops, SparseCore 0:
  683.6 132.4 all-gather.1
